TPU v7x, 512 devices: a whole 4x8x8 slice. The times are simulated.
512 devices in a mesh: wide: 64 (over y, x, z_lo), narrow: 8 (over z_hi, core).
Axes of the slice: x: 4, y: 8, z: 8 (z_hi: 4, z_lo: 2; z = z_hi * 2 + z_lo), core: 2. Of those that a mesh axis runs over, the one named last changes fastest.
Arguments:
- tval: bfloat16 [4096, 12, 128, 128], P(('wide', 'narrow')), may hold values from -0.16992188 to 0.16992188
- tcol: int32 [4096, 12], replicated, may hold values from 0 to 4095, as said below
- ocol: int32 [4096, 12], P(('wide', 'narrow')), may hold values from 0 to 4095, as said below
- basis: bfloat16 [524288, 128], P(('wide', 'narrow')), may hold values from -6 to 6
Outputs:
- projected: bfloat16 [524288, 128], P(('wide', 'narrow'))
- level: float32 [128, 128], replicated
Inputs may be any that keep to these rules, and one draw needn't show every extreme that they name: `tcol`: the 12 block columns of row i are distinct, include i, and each lies within cyclic distance 8 of i modulo 4096. `ocol`: the 12 block columns of row i are distinct, include i, and each lies within cyclic distance 8 of i modulo 4096.
All inputs are finite; a program needn't handle non-finite values.
Results may differ from a plain program's by a relative error of at most 0.0049.
Values may be sent and summed in bfloat16 or wider, within the bound.
No kernel may reach another device: no remote copies, remote signals or barrier semaphores. Data moves between devices by JAX's collectives and lax.ppermute only.
A program may use at most 64 MiB of HBM per device.

v0:
```python
import jax
import jax.numpy as jnp
from jax import lax
from jax.sharding import PartitionSpec as P


def with_halo(cells, sides, width):
    for axis, dim in sides:
        count = lax.axis_size(axis)
        head = lax.slice_in_dim(cells, 0, width, axis=dim)
        tail = lax.slice_in_dim(cells, cells.shape[dim] - width, cells.shape[dim], axis=dim)
        cells = jnp.concatenate(
            [
                lax.ppermute(tail, axis, [(i, (i + 1) % count) for i in range(count)]),
                cells,
                lax.ppermute(head, axis, [((i + 1) % count, i) for i in range(count)]),
            ],
            axis=dim,
        )
    return cells


def per_device(tval, tcol, ocol, basis):
    local = tval.shape[0]
    size = tval.shape[2]
    width = basis.shape[1]
    slots = tval.shape[1]
    devices = lax.axis_size(("wide", "narrow"))
    count = local * devices
    first = lax.axis_index(("wide", "narrow")) * local
    extended = with_halo(tval, ((("wide", "narrow"), 0),), local)
    basis_ext = with_halo(basis, ((("wide", "narrow"), 0),), local * size)
    basis_blocks = basis_ext.reshape(3 * local, size, width)
    slot_ids = jnp.arange(slots, dtype=jnp.int32)

    def one_row(index):
        glob = first + index
        cols = tcol[glob]
        places = (cols - first + local) % count
        pattern = tcol[cols]
        outcols = ocol[index]
        match = (pattern[None, :, :] == outcols[:, None, None]).astype(jnp.int32)
        which = jnp.sum(match * slot_ids[None, None, :], axis=2)
        valid = jnp.sum(match, axis=2).astype(jnp.bfloat16)
        chosen = extended[places[None, :], which]
        selected = chosen * valid[:, :, None, None]
        square = jnp.einsum(
            "sab,osbc->oac", tval[index], selected, preferred_element_type=jnp.float32
        ).astype(jnp.bfloat16)
        picked = basis_blocks[(outcols - first + local) % count]
        result = jnp.einsum("oac,ock->ak", square, picked, preferred_element_type=jnp.float32)
        return result.astype(jnp.bfloat16)

    projected = lax.map(one_row, jnp.arange(local, dtype=jnp.int32)).reshape(local * size, width)
    partial_level = jnp.dot(basis.T, projected, preferred_element_type=jnp.float32)
    level = lax.psum(partial_level, ("wide", "narrow"))
    level = level / jnp.sqrt(jnp.float32(count * size))
    return (projected, level)


def solution(mesh):
    return jax.shard_map(
        per_device,
        mesh=mesh,
        in_specs=(
            P(("wide", "narrow"), None, None, None),
            P(),
            P(("wide", "narrow"), None),
            P(("wide", "narrow"), None),
        ),
        out_specs=(P(("wide", "narrow"), None), P()),
        check_vma=False,
    )
```

profile of v0, /device:TPU:1, one launch (start us, length us, event | category | flops | bytes accessed | tf_op | source)
XLA Modules:
  0.0 650.9 jit_solution(2711179265260050932)
XLA Ops:
  7.2 7.2 %collective-permute-start = (bf16[8,12,128,128]{3,2,1,0:T(8,128)(2,1)}, bf16[8,12,128,128]{3,2,1,0:T(8,128)(2,1)}, u32[]{:S(2)}, u32[]{:S(2)}) collective-permute-start(bf16[8,12,128,128]{3,2,1,0:T(8,128)(2,1)} %param.6), channel_id=1, source_target_pairs={{0,1},{1,2},{2,3},{3,4},{4,5},{5,6},{6,7},{7,8},{8,9},{9,10},{10,1... | collective-permute-start | bytes 9437192 | tf_op jit(solution)/shard_map/ppermute | solution.py:14
  14.4 3.5 collective-permute-start.1
  17.9 3.0 collective-permute-start.2
  20.9 9.1 %collective-permute-start.3 = (bf16[1024,128]{1,0:T(8,128)(2,1)}, bf16[1024,128]{1,0:T(8,128)(2,1)S(1)}, u32[]{:S(2)}, u32[]{:S(2)}) collective-permute-start(bf16[1024,128]{1,0:T(8,128)(2,1)} %param.9), channel_id=1, source_target_pairs={{1,0},{2,1},{3,2},{4,3},{5,4},{6,5},{7,6},{8,7},{9,8},{10,9},{11,1... | collective-permute-start | bytes 786440 | tf_op jit(solution)/shard_map/ppermute | solution.py:16
  30.0 1.6 copy.12
  31.6 55.9 %collective-permute-done.2 = bf16[1024,128]{1,0:T(8,128)(2,1)S(1)} collective-permute-done((bf16[1024,128]{1,0:T(8,128)(2,1)}, bf16[1024,128]{1,0:T(8,128)(2,1)S(1)}, u32[]{:S(2)}, u32[]{:S(2)}) %collective-permute-start.2) | collective-permute-done | bytes 262176 | tf_op jit(solution)/shard_map/ppermute | solution.py:14
  87.5 6.0 collective-permute-done.3
  93.5 1.0 pad_maximum_fusion.1
  94.5 7.7 %pad_maximum_fusion = bf16[24,12,128,128]{3,2,1,0:T(8,128)(2,1)} fusion(bf16[8,12,128,128]{3,2,1,0:T(8,128)(2,1)} %collective-permute-done.1, bf16[8,12,128,128]{3,2,1,0:T(8,128)(2,1)} %param.6, bf16[8,12,128,128]{3,2,1,0:T(8,128)(2,1)} %collective-permute-done), kind=kLoop, calls=%fused_computation.47 | loop fusion | flops 9437184 | bytes 18874368 | tf_op jit(solution)/shard_map/concatenate | solution.py:12
  102.2 269.6 %while.13 = (s32[]{:T(128)}, bf16[8,128,128]{2,1,0:T(8,128)(2,1)}, s32[8]{0:T(128)S(1)}, s32[]{:T(128)}, s32[4096,12]{1,0:T(8,128)S(1)}, /*index=5*/s32[8,12]{1,...) while((s32[]{:T(128)}, bf16[8,128,128]{2,1,0:T(8,128)(2,1)}, ...), condition=%wide.region_3.4_spmd.clone, body=%wide.region_0.3_spmd.clone.sunk | while | flops 656895552 | bytes 25215700 | solution.py:54
  105.4 0.7 fusion.62
  106.6 0.7 fusion.63
  108.0 15.8 %gather_fusion.2 = bf16[144,128,128]{2,1,0:T(8,128)(2,1)} fusion(bf16[24,12,128,128]{3,2,1,0:T(8,128)(2,1)} %get-tuple-element.305, s32[144]{0:T(256)S(1)} %reshape.191), kind=kCustom, calls=%fused_computation.1.clone.clone.1 | custom fusion | bytes 9438336 | tf_op jit(solution)/shard_map/while/body/eval_jaxpr/gather | solution.py:45
  123.8 6.7 %copy.17 = bf16[12,12,128,128]{2,3,1,0:T(8,128)(2,1)} copy(bf16[12,12,128,128]{3,2,1,0:T(8,128)(2,1)} %bitcast.95) | data formatting | bytes 9437184 | tf_op jit(solution)/shard_map/while/body/eval_jaxpr/gather | solution.py:45
  131.1 4.8 fusion.66
  140.3 0.7 fusion.63
  141.7 15.8 %gather_fusion.2 = bf16[144,128,128]{2,1,0:T(8,128)(2,1)} fusion(bf16[24,12,128,128]{3,2,1,0:T(8,128)(2,1)} %get-tuple-element.305, s32[144]{0:T(256)S(1)} %reshape.191), kind=kCustom, calls=%fused_computation.1.clone.clone.1 | custom fusion | bytes 9438336 | tf_op jit(solution)/shard_map/while/body/eval_jaxpr/gather | solution.py:45
  157.5 6.7 %copy.17 = bf16[12,12,128,128]{2,3,1,0:T(8,128)(2,1)} copy(bf16[12,12,128,128]{3,2,1,0:T(8,128)(2,1)} %bitcast.95) | data formatting | bytes 9437184 | tf_op jit(solution)/shard_map/while/body/eval_jaxpr/gather | solution.py:45
  164.8 4.8 fusion.66
  174.0 0.7 fusion.63
  175.4 15.8 %gather_fusion.2 = bf16[144,128,128]{2,1,0:T(8,128)(2,1)} fusion(bf16[24,12,128,128]{3,2,1,0:T(8,128)(2,1)} %get-tuple-element.305, s32[144]{0:T(256)S(1)} %reshape.191), kind=kCustom, calls=%fused_computation.1.clone.clone.1 | custom fusion | bytes 9438336 | tf_op jit(solution)/shard_map/while/body/eval_jaxpr/gather | solution.py:45
  191.2 6.7 %copy.17 = bf16[12,12,128,128]{2,3,1,0:T(8,128)(2,1)} copy(bf16[12,12,128,128]{3,2,1,0:T(8,128)(2,1)} %bitcast.95) | data formatting | bytes 9437184 | tf_op jit(solution)/shard_map/while/body/eval_jaxpr/gather | solution.py:45
  198.5 4.8 fusion.66
  207.7 0.7 fusion.63
  209.1 15.8 %gather_fusion.2 = bf16[144,128,128]{2,1,0:T(8,128)(2,1)} fusion(bf16[24,12,128,128]{3,2,1,0:T(8,128)(2,1)} %get-tuple-element.305, s32[144]{0:T(256)S(1)} %reshape.191), kind=kCustom, calls=%fused_computation.1.clone.clone.1 | custom fusion | bytes 9438336 | tf_op jit(solution)/shard_map/while/body/eval_jaxpr/gather | solution.py:45
  224.9 6.7 %copy.17 = bf16[12,12,128,128]{2,3,1,0:T(8,128)(2,1)} copy(bf16[12,12,128,128]{3,2,1,0:T(8,128)(2,1)} %bitcast.95) | data formatting | bytes 9437184 | tf_op jit(solution)/shard_map/while/body/eval_jaxpr/gather | solution.py:45
  232.2 4.8 fusion.66
  241.4 0.7 fusion.63
  242.8 15.8 %gather_fusion.2 = bf16[144,128,128]{2,1,0:T(8,128)(2,1)} fusion(bf16[24,12,128,128]{3,2,1,0:T(8,128)(2,1)} %get-tuple-element.305, s32[144]{0:T(256)S(1)} %reshape.191), kind=kCustom, calls=%fused_computation.1.clone.clone.1 | custom fusion | bytes 9438336 | tf_op jit(solution)/shard_map/while/body/eval_jaxpr/gather | solution.py:45
  258.6 6.7 %copy.17 = bf16[12,12,128,128]{2,3,1,0:T(8,128)(2,1)} copy(bf16[12,12,128,128]{3,2,1,0:T(8,128)(2,1)} %bitcast.95) | data formatting | bytes 9437184 | tf_op jit(solution)/shard_map/while/body/eval_jaxpr/gather | solution.py:45
  265.9 4.8 fusion.66
  273.8 0.7 fusion.62
  275.1 0.7 fusion.63
  276.5 15.8 %gather_fusion.2 = bf16[144,128,128]{2,1,0:T(8,128)(2,1)} fusion(bf16[24,12,128,128]{3,2,1,0:T(8,128)(2,1)} %get-tuple-element.305, s32[144]{0:T(256)S(1)} %reshape.191), kind=kCustom, calls=%fused_computation.1.clone.clone.1 | custom fusion | bytes 9438336 | tf_op jit(solution)/shard_map/while/body/eval_jaxpr/gather | solution.py:45
  292.3 6.7 %copy.17 = bf16[12,12,128,128]{2,3,1,0:T(8,128)(2,1)} copy(bf16[12,12,128,128]{3,2,1,0:T(8,128)(2,1)} %bitcast.95) | data formatting | bytes 9437184 | tf_op jit(solution)/shard_map/while/body/eval_jaxpr/gather | solution.py:45
  299.7 4.8 fusion.66
  308.8 0.7 fusion.63
  310.2 15.8 %gather_fusion.2 = bf16[144,128,128]{2,1,0:T(8,128)(2,1)} fusion(bf16[24,12,128,128]{3,2,1,0:T(8,128)(2,1)} %get-tuple-element.305, s32[144]{0:T(256)S(1)} %reshape.191), kind=kCustom, calls=%fused_computation.1.clone.clone.1 | custom fusion | bytes 9438336 | tf_op jit(solution)/shard_map/while/body/eval_jaxpr/gather | solution.py:45
  326.1 6.7 %copy.17 = bf16[12,12,128,128]{2,3,1,0:T(8,128)(2,1)} copy(bf16[12,12,128,128]{3,2,1,0:T(8,128)(2,1)} %bitcast.95) | data formatting | bytes 9437184 | tf_op jit(solution)/shard_map/while/body/eval_jaxpr/gather | solution.py:45
  333.4 4.8 fusion.66
  342.6 0.7 fusion.63
  343.9 15.8 %gather_fusion.2 = bf16[144,128,128]{2,1,0:T(8,128)(2,1)} fusion(bf16[24,12,128,128]{3,2,1,0:T(8,128)(2,1)} %get-tuple-element.305, s32[144]{0:T(256)S(1)} %reshape.191), kind=kCustom, calls=%fused_computation.1.clone.clone.1 | custom fusion | bytes 9438336 | tf_op jit(solution)/shard_map/while/body/eval_jaxpr/gather | solution.py:45
  359.8 6.7 %copy.17 = bf16[12,12,128,128]{2,3,1,0:T(8,128)(2,1)} copy(bf16[12,12,128,128]{3,2,1,0:T(8,128)(2,1)} %bitcast.95) | data formatting | bytes 9437184 | tf_op jit(solution)/shard_map/while/body/eval_jaxpr/gather | solution.py:45
  367.1 4.8 fusion.66
  371.9 1.9 convolution_bitcast_fusion
  373.7 268.7 %all-reduce.2.cloned.1.call-done = f32[128,128]{0,1:T(8,128)} async-done(((f32[128,128]{0,1:T(8,128)}), f32[128,128]{0,1:T(8,128)}) %all-reduce.2.cloned.1.call-update) | async-done | bytes 65552 | tf_op jit(solution)/shard_map/psum | solution.py:56
  642.5 0.8 broadcast_multiply_fusion
  643.3 0.7 copy.13
  (86 shorter events, 24.0 us)
Async XLA Ops:
  7.2 635.3 %all-reduce.2.cloned.1.call-start = ((), (), s32[]{:S(2)}) async-start(), calls=%async_computation | async-start | bytes 131072 | tf_op jit(solution)/shard_map/psum | solution.py:56
  7.2 87.3 %collective-permute-start = (bf16[8,12,128,128]{3,2,1,0:T(8,128)(2,1)}, bf16[8,12,128,128]{3,2,1,0:T(8,128)(2,1)}, u32[]{:S(2)}, u32[]{:S(2)}) collective-permute-start(bf16[8,12,128,128]{3,2,1,0:T(8,128)(2,1)} %param.6), channel_id=1, source_target_pairs={{0,1},{1,2},{2,3},{3,4},{4,5},{5,6},{6,7},{7,8},{8,9},{9,10},{10,1... | collective-permute-start | bytes 9437192 | tf_op jit(solution)/shard_map/ppermute | solution.py:14
  14.4 80.1 %collective-permute-start.1 = (bf16[8,12,128,128]{3,2,1,0:T(8,128)(2,1)}, bf16[8,12,128,128]{3,2,1,0:T(8,128)(2,1)}, u32[]{:S(2)}, u32[]{:S(2)}) collective-permute-start(bf16[8,12,128,128]{3,2,1,0:T(8,128)(2,1)} %param.6), channel_id=1, source_target_pairs={{1,0},{2,1},{3,2},{4,3},{5,4},{6,5},{7,6},{8,7},{9,8},{10,9},{11,1... | collective-permute-start | bytes 9437192 | tf_op jit(solution)/shard_map/ppermute | solution.py:16
  17.9 69.6 %collective-permute-start.2 = (bf16[1024,128]{1,0:T(8,128)(2,1)}, bf16[1024,128]{1,0:T(8,128)(2,1)S(1)}, u32[]{:S(2)}, u32[]{:S(2)}) collective-permute-start(bf16[1024,128]{1,0:T(8,128)(2,1)} %param.9), channel_id=1, source_target_pairs={{0,1},{1,2},{2,3},{3,4},{4,5},{5,6},{6,7},{7,8},{8,9},{9,10},{10,1... | collective-permute-start | bytes 786440 | tf_op jit(solution)/shard_map/ppermute | solution.py:14
  20.9 72.6 %collective-permute-start.3 = (bf16[1024,128]{1,0:T(8,128)(2,1)}, bf16[1024,128]{1,0:T(8,128)(2,1)S(1)}, u32[]{:S(2)}, u32[]{:S(2)}) collective-permute-start(bf16[1024,128]{1,0:T(8,128)(2,1)} %param.9), channel_id=1, source_target_pairs={{1,0},{2,1},{3,2},{4,3},{5,4},{6,5},{7,6},{8,7},{9,8},{10,9},{11,1... | collective-permute-start | bytes 786440 | tf_op jit(solution)/shard_map/ppermute | solution.py:16
  102.2 269.6 %copy-start = (bf16[1024,128]{1,0:T(8,128)(2,1)S(1)}, bf16[1024,128]{1,0:T(8,128)(2,1)}, u32[]{:S(2)}) copy-start(bf16[1024,128]{1,0:T(8,128)(2,1)} %param.9) | copy-start | bytes 786436
Sparse Core Ops, SparseCore 0:
  373.8 268.5 all-reduce.1
where the time goes:
time: 653 us; the launch traced here: 651 us
  waiting for transfers between devices  331 us (51%)
  local copies, waits for them, and re-layouts  197 us (30%)
  matrix products  40 us (6%)
  other arithmetic  25.5 us (4%)
  starting transfers between devices  22.8 us (3%)
  loops' own time  20.3 us (3%)
  between operations  14.1 us (2%)
    psum x1, waiting for transfers between devices, per_device(): level = lax.psum(partial_level, ('wide', 'narrow'))  269 us
    gather x16, local copies, waits for them, and re-layouts, one_row(): chosen = extended[places[None, :], which]  180 us
    ppermute x2, waiting for transfers between devices, with_halo(): lax.ppermute(tail, axis, [(i, (i + 1) % count) for i in range(count)])  55.9 us
    dot_general x8, matrix products, one_row(): jnp.einsum('oac,ock->ak', square, picked, preferred_element_type=jnp.floa...  38.2 us
    another operation x1, loops' own time, per_device(): lax.map(one_row, jnp.arange(local, dtype=jnp.int32))  20.3 us
  transfers between devices with their start and end apart: 5, of which 3 were waited for; matrix products, arithmetic and copies ran while one was open for 0% of the time, Pallas kernels for 0%

commit v1 on v0

--- a/solution.py
+++ b/solution.py
@@ -2,6 +2,12 @@
 import jax.numpy as jnp
 from jax import lax
 from jax.sharding import PartitionSpec as P
+
+
+def add_all(array, axis):
+    pieces = lax.all_gather(array, axis, axis=0, tiled=False)
+    result = pieces.sum(axis=0)
+    return result
 
 
 def with_halo(cells, sides, width):
@@ -53,7 +59,7 @@
 
     projected = lax.map(one_row, jnp.arange(local, dtype=jnp.int32)).reshape(local * size, width)
     partial_level = jnp.dot(basis.T, projected, preferred_element_type=jnp.float32)
-    level = lax.psum(partial_level, ("wide", "narrow"))
+    level = add_all(partial_level, ("wide", "narrow"))
     level = level / jnp.sqrt(jnp.float32(count * size))
     return (projected, level)
 

time: 653 us -> 1290 us (1.98)
  waiting for transfers between devices: 331 us -> 949 us
  local copies, waits for them, and re-layouts: 197 us -> 215 us
    all_gather x0 -> x1, waiting for transfers between devices: none -> 891 us  [add_all(): pieces = lax.all_gather(array, axis, axis=0, tiled=False)]
    psum x1 -> x0, waiting for transfers between devices: 269 us -> none  [per_device(): level = lax.psum(partial_level, ('wide', 'narrow'))]
    ppermute x2, waiting for transfers between devices: 55.9 us -> 0.01 us  [with_halo(): lax.ppermute(tail, axis, [(i, (i + 1) % count) for i in range(count)])]
    ppermute x2, waiting for transfers between devices: 6 us -> 57.3 us  [with_halo(): lax.ppermute(head, axis, [((i + 1) % count, i) for i in range(count)])]
    unnamed x4 -> x5, local copies, waits for them, and re-layouts: 2.3 us -> 19.5 us
  transfers between devices with their start and end apart: 5 -> 5, of which waited for: 3 -> 2; matrix products, arithmetic and copies ran while one was open for 0% -> 0% of each run, Pallas kernels for 0% -> 0%
where the time goes in v1:
time: 1290 us
  waiting for transfers between devices  949 us (74%)
  local copies, waits for them, and re-layouts  215 us (17%)
  matrix products  40.1 us (3%)
  other arithmetic  28.6 us (2%)
  starting transfers between devices  22.8 us (2%)
  loops' own time  20.4 us (2%)
  between operations  14.1 us (1%)
    all_gather x1, waiting for transfers between devices, add_all(): pieces = lax.all_gather(array, axis, axis=0, tiled=False)  891 us
    gather x16, local copies, waits for them, and re-layouts, one_row(): chosen = extended[places[None, :], which]  180 us
    ppermute x2, waiting for transfers between devices, with_halo(): lax.ppermute(head, axis, [((i + 1) % count, i) for i in range(count)])  57.3 us
    dot_general x8, matrix products, one_row(): jnp.einsum('oac,ock->ak', square, picked, preferred_element_type=jnp.floa...  38.2 us
  transfers between devices with their start and end apart: 5, of which 2 were waited for; matrix products, arithmetic and copies ran while one was open for 0% of the time, Pallas kernels for 0%

profile of v1, /device:TPU:1, one launch (start us, length us, event | category | flops | bytes accessed | tf_op | source)
XLA Modules:
  0.0 1289.4 jit_solution(3569394387608713950)
XLA Ops:
  7.2 8.8 collective-permute-start.1
  16.0 1.9 collective-permute-start
  17.9 10.1 collective-permute-start.3
  28.1 1.9 collective-permute-start.2
  30.0 1.6 copy.14
  31.6 57.3 %collective-permute-done.3 = bf16[1024,128]{1,0:T(8,128)(2,1)S(1)} collective-permute-done((bf16[1024,128]{1,0:T(8,128)(2,1)}, bf16[1024,128]{1,0:T(8,128)(2,1)S(1)}, u32[]{:S(2)}, u32[]{:S(2)}) %collective-permute-start.3) | collective-permute-done | bytes 262176 | tf_op jit(solution)/shard_map/ppermute | solution.py:22
  88.9 1.0 pad_maximum_fusion.1
  90.0 7.7 pad_maximum_fusion
  97.7 269.7 %while.13 = (s32[]{:T(128)}, bf16[8,128,128]{2,1,0:T(8,128)(2,1)}, s32[8]{0:T(128)S(1)}, s32[]{:T(128)}, s32[4096,12]{1,0:T(8,128)S(1)}, /*index=5*/s32[8,12]{1,...) while((s32[]{:T(128)}, bf16[8,128,128]{2,1,0:T(8,128)(2,1)}, ...), condition=%wide.region_3.4_spmd.clone, body=%wide.region_0.3_spmd.clone.sunk | while | flops 656895552 | bytes 25215200 | solution.py:60
  100.8 0.7 fusion.63
  101.5 0.7 fusion.62
  104.1 15.8 %gather_fusion.2 = bf16[144,128,128]{2,1,0:T(8,128)(2,1)} fusion(bf16[24,12,128,128]{3,2,1,0:T(8,128)(2,1)} %get-tuple-element.312, s32[144]{0:T(256)S(1)} %reshape.192), kind=kCustom, calls=%fused_computation.1.clone.clone.1 | custom fusion | bytes 9438336 | tf_op jit(solution)/shard_map/while/body/eval_jaxpr/gather | solution.py:51
  119.9 6.7 copy.20
  126.6 4.8 fusion.66
  134.5 0.7 fusion.63
  135.2 0.7 fusion.62
  137.8 15.8 %gather_fusion.2 = bf16[144,128,128]{2,1,0:T(8,128)(2,1)} fusion(bf16[24,12,128,128]{3,2,1,0:T(8,128)(2,1)} %get-tuple-element.312, s32[144]{0:T(256)S(1)} %reshape.192), kind=kCustom, calls=%fused_computation.1.clone.clone.1 | custom fusion | bytes 9438336 | tf_op jit(solution)/shard_map/while/body/eval_jaxpr/gather | solution.py:51
  153.6 6.7 copy.20
  160.3 4.8 fusion.66
  168.2 0.7 fusion.63
  171.5 15.8 %gather_fusion.2 = bf16[144,128,128]{2,1,0:T(8,128)(2,1)} fusion(bf16[24,12,128,128]{3,2,1,0:T(8,128)(2,1)} %get-tuple-element.312, s32[144]{0:T(256)S(1)} %reshape.192), kind=kCustom, calls=%fused_computation.1.clone.clone.1 | custom fusion | bytes 9438336 | tf_op jit(solution)/shard_map/while/body/eval_jaxpr/gather | solution.py:51
  187.3 6.7 copy.20
  194.0 4.8 fusion.66
  201.9 0.7 fusion.63
  205.2 15.8 %gather_fusion.2 = bf16[144,128,128]{2,1,0:T(8,128)(2,1)} fusion(bf16[24,12,128,128]{3,2,1,0:T(8,128)(2,1)} %get-tuple-element.312, s32[144]{0:T(256)S(1)} %reshape.192), kind=kCustom, calls=%fused_computation.1.clone.clone.1 | custom fusion | bytes 9438336 | tf_op jit(solution)/shard_map/while/body/eval_jaxpr/gather | solution.py:51
  221.1 6.7 copy.20
  227.7 4.8 fusion.66
  235.6 0.7 fusion.63
  238.9 15.8 %gather_fusion.2 = bf16[144,128,128]{2,1,0:T(8,128)(2,1)} fusion(bf16[24,12,128,128]{3,2,1,0:T(8,128)(2,1)} %get-tuple-element.312, s32[144]{0:T(256)S(1)} %reshape.192), kind=kCustom, calls=%fused_computation.1.clone.clone.1 | custom fusion | bytes 9438336 | tf_op jit(solution)/shard_map/while/body/eval_jaxpr/gather | solution.py:51
  254.8 6.7 copy.20
  261.4 4.8 fusion.66
  269.3 0.7 fusion.63
  272.6 15.8 %gather_fusion.2 = bf16[144,128,128]{2,1,0:T(8,128)(2,1)} fusion(bf16[24,12,128,128]{3,2,1,0:T(8,128)(2,1)} %get-tuple-element.312, s32[144]{0:T(256)S(1)} %reshape.192), kind=kCustom, calls=%fused_computation.1.clone.clone.1 | custom fusion | bytes 9438336 | tf_op jit(solution)/shard_map/while/body/eval_jaxpr/gather | solution.py:51
  288.5 6.7 copy.20
  295.2 4.8 fusion.66
  303.1 0.7 fusion.63
  306.4 15.8 %gather_fusion.2 = bf16[144,128,128]{2,1,0:T(8,128)(2,1)} fusion(bf16[24,12,128,128]{3,2,1,0:T(8,128)(2,1)} %get-tuple-element.312, s32[144]{0:T(256)S(1)} %reshape.192), kind=kCustom, calls=%fused_computation.1.clone.clone.1 | custom fusion | bytes 9438336 | tf_op jit(solution)/shard_map/while/body/eval_jaxpr/gather | solution.py:51
  322.2 6.7 copy.20
  328.9 4.8 fusion.66
  336.8 0.7 fusion.63
  340.1 15.8 %gather_fusion.2 = bf16[144,128,128]{2,1,0:T(8,128)(2,1)} fusion(bf16[24,12,128,128]{3,2,1,0:T(8,128)(2,1)} %get-tuple-element.312, s32[144]{0:T(256)S(1)} %reshape.192), kind=kCustom, calls=%fused_computation.1.clone.clone.1 | custom fusion | bytes 9438336 | tf_op jit(solution)/shard_map/while/body/eval_jaxpr/gather | solution.py:51
  355.9 6.7 copy.20
  362.6 4.8 fusion.66
  367.4 1.9 convolution_bitcast_fusion
  369.3 891.3 %all-gather.3.cloned.1.call-done = f32[65536,128]{0,1:T(8,128)} async-done(((f32[128,128]{0,1:T(8,128)}), f32[65536,128]{0,1:T(8,128)}) %all-gather.3.cloned.1.call-update) | async-done | bytes 33554448 | tf_op jit(solution)/shard_map/all_gather | solution.py:8
  1260.6 17.2 %copy.18 = f32[16,8,512,128]{3,2,1,0:T(8,128)S(1)} copy(f32[16,8,512,128]{3,1,2,0:T(8,128)} %bitcast.101) | data formatting | bytes 67108864
  1277.8 4.0 bitcast_reduce_fusion
  1281.8 0.7 copy.15
  (88 shorter events, 24.1 us)
Async XLA Ops:
  7.2 1253.4 %all-gather.3.cloned.1.call-start = ((), (), s32[]{:S(2)}) async-start(), calls=%async_computation | async-start | bytes 33619968 | tf_op jit(solution)/shard_map/all_gather | solution.py:8
  7.2 82.7 %collective-permute-start.1 = (bf16[8,12,128,128]{3,2,1,0:T(8,128)(2,1)}, bf16[8,12,128,128]{3,2,1,0:T(8,128)(2,1)}, u32[]{:S(2)}, u32[]{:S(2)}) collective-permute-start(bf16[8,12,128,128]{3,2,1,0:T(8,128)(2,1)} %param.6), channel_id=1, source_target_pairs={{1,0},{2,1},{3,2},{4,3},{5,4},{6,5},{7,6},{8,7},{9,8},{10,9},{11,1... | collective-permute-start | bytes 9437192 | tf_op jit(solution)/shard_map/ppermute | solution.py:22
  16.0 73.9 %collective-permute-start = (bf16[8,12,128,128]{3,2,1,0:T(8,128)(2,1)}, bf16[8,12,128,128]{3,2,1,0:T(8,128)(2,1)}, u32[]{:S(2)}, u32[]{:S(2)}) collective-permute-start(bf16[8,12,128,128]{3,2,1,0:T(8,128)(2,1)} %param.6), channel_id=1, source_target_pairs={{0,1},{1,2},{2,3},{3,4},{4,5},{5,6},{6,7},{7,8},{8,9},{9,10},{10,1... | collective-permute-start | bytes 9437192 | tf_op jit(solution)/shard_map/ppermute | solution.py:20
  17.9 71.0 %collective-permute-start.3 = (bf16[1024,128]{1,0:T(8,128)(2,1)}, bf16[1024,128]{1,0:T(8,128)(2,1)S(1)}, u32[]{:S(2)}, u32[]{:S(2)}) collective-permute-start(bf16[1024,128]{1,0:T(8,128)(2,1)} %param.9), channel_id=1, source_target_pairs={{1,0},{2,1},{3,2},{4,3},{5,4},{6,5},{7,6},{8,7},{9,8},{10,9},{11,1... | collective-permute-start | bytes 786440 | tf_op jit(solution)/shard_map/ppermute | solution.py:22
  28.1 60.9 %collective-permute-start.2 = (bf16[1024,128]{1,0:T(8,128)(2,1)}, bf16[1024,128]{1,0:T(8,128)(2,1)S(1)}, u32[]{:S(2)}, u32[]{:S(2)}) collective-permute-start(bf16[1024,128]{1,0:T(8,128)(2,1)} %param.9), channel_id=1, source_target_pairs={{0,1},{1,2},{2,3},{3,4},{4,5},{5,6},{6,7},{7,8},{8,9},{9,10},{10,1... | collective-permute-start | bytes 786440 | tf_op jit(solution)/shard_map/ppermute | solution.py:20
  97.7 269.7 %copy-start = (bf16[1024,128]{1,0:T(8,128)(2,1)S(1)}, bf16[1024,128]{1,0:T(8,128)(2,1)}, u32[]{:S(2)}) copy-start(bf16[1024,128]{1,0:T(8,128)(2,1)} %param.9) | copy-start | bytes 786436
Sparse Core Ops, SparseCore 0:
  369.4 891.1 all-gather.2
